TPU v7x, 32 devices: a whole 2x2x4 slice. The times are simulated.
32 devices in a mesh: dp: 4 (over y, core), expert: 8 (over z, x).
Axes of the slice: x: 2, y: 2, z: 4, core: 2. Of those that a mesh axis runs over, the one named last changes fastest.
Arguments:
- tokens: bfloat16 [4096, 2048], P(('dp', 'expert')), may hold values from -6 to 6
- routes: int32 [4096, 4], P(('dp', 'expert')), may hold values from 0 to 7, all different within a row; in each aligned block of 128 rows (0 to 127, 128 to 255, ...) at most 96 rows name the same one
- combine: float32 [4096, 4], P(('dp', 'expert')), may hold values from 0.2 to 1
- cotangent: bfloat16 [4096, 2048], P(('dp', 'expert')), may hold values from -1.5 to 1.5
- w_gate: bfloat16 [8, 2048, 768], P('expert'), may hold values from -0.125 to 0.125
- w_up: bfloat16 [8, 2048, 768], P('expert'), may hold values from -0.125 to 0.125
- w_down: bfloat16 [8, 768, 2048], P('expert'), may hold values from -0.21875 to 0.21875
Outputs:
- output: bfloat16 [4096, 2048], P(('dp', 'expert'))
- d_tokens: bfloat16 [4096, 2048], P(('dp', 'expert'))
- d_combine: float32 [4096, 4], P(('dp', 'expert'))
- d_w_gate: bfloat16 [8, 2048, 768], P('expert', 'dp')
- d_w_up: bfloat16 [8, 2048, 768], P('expert', 'dp')
- d_w_down: bfloat16 [8, 768, 2048], P('expert', None, 'dp')
Inputs may be any that keep to these rules, and one draw needn't show every extreme that they name: `routes`: each row names 4 different experts. In the rows of one device (aligned blocks of 128 rows) no expert is named by more than 96 rows, a bound that some block reaches.
All inputs are finite; a program needn't handle non-finite values.
Results may differ from a plain program's by a relative error of at most 0.014.
Values may be sent and summed in bfloat16 or wider, within the bound.
No kernel may reach another device: no remote copies, remote signals or barrier semaphores. Data moves between devices by JAX's collectives and lax.ppermute only.
A program may use at most 128 MiB of HBM per device.

v0:
```python
import jax
import jax.numpy as jnp
from jax import lax
from jax.sharding import PartitionSpec as P


def slot_map(routes, experts, capacity):
    flat_ids = routes.reshape(-1)
    onehot = (flat_ids[:, None] == jnp.arange(experts, dtype=jnp.int32)[None, :]).astype(jnp.int32)
    before = jnp.cumsum(onehot, axis=0) - onehot
    slots = jnp.sum(before * onehot, axis=1)
    target = flat_ids * capacity + slots
    source = (
        jnp.full((experts * capacity,), -1, jnp.int32)
        .at[target]
        .set(jnp.arange(flat_ids.shape[0], dtype=jnp.int32))
    )
    return (target, source)


def per_device(tokens, routes, combine, cotangent, w_gate, w_up, w_down):
    tok_rows, features = tokens.shape
    per_token = routes.shape[1]
    groups = lax.axis_size("expert")
    local_exp = w_gate.shape[0]
    experts = local_exp * groups
    capacity = 3 * tok_rows * per_token // (2 * experts)
    target, source = slot_map(routes, experts, capacity)
    filled = (source >= 0)[:, None]
    pair_index = jnp.maximum(source, 0)
    owner_row = pair_index // per_token
    outgoing = jnp.where(filled, tokens[owner_row], jnp.zeros((), jnp.bfloat16))
    outgoing = outgoing.reshape(groups, local_exp, capacity, features)
    cot_float = cotangent.astype(jnp.float32)
    scaled = (combine[:, :, None] * cot_float[:, None, :]).reshape(tok_rows * per_token, features)
    outgoing_grad = jnp.where(filled, scaled[pair_index], 0.0).astype(jnp.bfloat16)
    outgoing_grad = outgoing_grad.reshape(groups, local_exp, capacity, features)
    arrived = lax.all_to_all(outgoing, "expert", split_axis=0, concat_axis=0, tiled=True)
    gate_pre = jnp.einsum("secd,edf->secf", arrived, w_gate, preferred_element_type=jnp.float32)
    up_pre = jnp.einsum("secd,edf->secf", arrived, w_up, preferred_element_type=jnp.float32)
    activated = jax.nn.silu(gate_pre)
    hidden = (activated * up_pre).astype(jnp.bfloat16)
    produced = jnp.einsum(
        "secf,efd->secd", hidden, w_down, preferred_element_type=jnp.float32
    ).astype(jnp.bfloat16)
    returned = lax.all_to_all(produced, "expert", split_axis=0, concat_axis=0, tiled=True)
    d_in = lax.all_to_all(outgoing_grad, "expert", split_axis=0, concat_axis=0, tiled=True)
    d_hidden = jnp.einsum("secd,efd->secf", d_in, w_down, preferred_element_type=jnp.float32)
    part_down = jnp.einsum("secf,secd->efd", hidden, d_in, preferred_element_type=jnp.float32)
    sigmoid_g = jax.nn.sigmoid(gate_pre)
    d_gate = (d_hidden * up_pre * sigmoid_g * (1.0 + gate_pre * (1.0 - sigmoid_g))).astype(
        jnp.bfloat16
    )
    d_up = (d_hidden * activated).astype(jnp.bfloat16)
    part_gate = jnp.einsum("secd,secf->edf", arrived, d_gate, preferred_element_type=jnp.float32)
    part_up = jnp.einsum("secd,secf->edf", arrived, d_up, preferred_element_type=jnp.float32)
    d_rows = (
        jnp.einsum("secf,edf->secd", d_gate, w_gate, preferred_element_type=jnp.float32)
        + jnp.einsum("secf,edf->secd", d_up, w_up, preferred_element_type=jnp.float32)
    ).astype(jnp.bfloat16)
    back = lax.all_to_all(d_rows, "expert", split_axis=0, concat_axis=0, tiled=True)
    per_slot = returned.reshape(experts * capacity, features)[target]
    per_slot = per_slot.reshape(tok_rows, per_token, features).astype(jnp.float32)
    output = jnp.sum(combine[:, :, None] * per_slot, axis=1).astype(jnp.bfloat16)
    d_combine = jnp.sum(per_slot * cot_float[:, None, :], axis=2)
    back_slot = back.reshape(experts * capacity, features)[target]
    back_slot = back_slot.reshape(tok_rows, per_token, features).astype(jnp.float32)
    d_tokens = jnp.sum(back_slot, axis=1).astype(jnp.bfloat16)
    sum_gate, sum_up, sum_down = (
        lax.psum_scatter(
            part_gate.astype(jnp.bfloat16), "dp", scatter_dimension=1, tiled=True
        ).astype(jnp.float32),
        lax.psum_scatter(
            part_up.astype(jnp.bfloat16), "dp", scatter_dimension=1, tiled=True
        ).astype(jnp.float32),
        lax.psum_scatter(
            part_down.astype(jnp.bfloat16), "dp", scatter_dimension=2, tiled=True
        ).astype(jnp.float32),
    )
    d_w_down = sum_down.astype(jnp.bfloat16)
    return (
        output,
        d_tokens,
        d_combine,
        sum_gate.astype(jnp.bfloat16),
        sum_up.astype(jnp.bfloat16),
        d_w_down,
    )


def solution(mesh):
    return jax.shard_map(
        per_device,
        mesh=mesh,
        in_specs=(
            P(("dp", "expert"), None),
            P(("dp", "expert"), None),
            P(("dp", "expert"), None),
            P(("dp", "expert"), None),
            P("expert", None, None),
            P("expert", None, None),
            P("expert", None, None),
        ),
        out_specs=(
            P(("dp", "expert"), None),
            P(("dp", "expert"), None),
            P(("dp", "expert"), None),
            P("expert", "dp", None),
            P("expert", "dp", None),
            P("expert", None, "dp"),
        ),
        check_vma=False,
    )
```

profile of v0, /device:TPU:0, one launch (start us, length us, event | category | flops | bytes accessed | tf_op | source)
XLA Modules:
  0.0 413.5 jit_solution(7218778556772040950)
XLA Ops:
  9.0 1.1 reduce-window.6
  10.8 2.4 scatter_custom_fusion
  14.1 4.2 %mul.87 = f32[128,4,2048]{2,1,0:T(4,128)} broadcast(bf16[128,2048]{1,0:T(8,128)(2,1)} %param.10), dimensions={0,2} | broadcast | bytes 4718592 | tf_op jit(solution)/shard_map/mul | solution.py:35
  18.3 5.3 %mul.88 = f32[512,2048]{1,0:T(8,128)} reshape(f32[128,4,2048]{2,1,0:T(4,128)} %mul.87) | data formatting | bytes 8388608 | tf_op jit(solution)/shard_map/mul | solution.py:35
  23.7 3.8 broadcast_multiply_fusion
  27.5 9.0 %gather_fusion.2 = bf16[768,2048]{1,0:T(8,128)(2,1)} fusion(bf16[512,2048]{1,0:T(8,128)(2,1)} %broadcast_multiply_fusion, s32[1024]{0:T(1024)S(1)} %get-tuple-element.21), kind=kCustom, calls=%fused_computation.2 | custom fusion | bytes 6294528 | tf_op jit(solution)/shard_map/gather | solution.py:36
  36.4 8.3 %gather_fusion = bf16[768,2048]{1,0:T(8,128)(2,1)} fusion(bf16[128,2048]{1,0:T(8,128)(2,1)} %param.7, s32[1024]{0:T(1024)S(1)} %get-tuple-element.22), kind=kCustom, calls=%fused_computation | custom fusion | bytes 6294528 | tf_op jit(solution)/shard_map/gather | solution.py:32
  44.7 5.2 %select_convert_fusion = (bf16[8,1,96,2048]{3,2,1,0:T(8,128)(2,1)}, bf16[8,1,96,2048]{3,2,1,0:T(8,128)(2,1)S(1)}) fusion(bf16[8,1,96,2048]{3,2,1,0:T(8,128)(2,1)} %bitcast.165, pred[8,96]{1,0:T(8,128)(4,1)S(1)} %broadcast_in_dim.43, bf16[8,1,96,2048]{3,2,1,0:T(8,128)(2,1)} %bitcast.166), kind=kLoop, calls=%fused_computation.9 | loop fusion | flops 3145728 | bytes 12583680 | tf_op jit(solution)/shard_map/convert_element_type | solution.py:36
  49.9 77.9 %all_to_all.20 = bf16[8,1,96,2048]{3,2,1,0:T(8,128)(2,1)} all-to-all(bf16[8,1,96,2048]{3,2,1,0:T(8,128)(2,1)S(1)} %get-tuple-element.20), channel_id=1, replica_groups=mesh['dp'=4,'expert'=8] {'expert'}, dimensions={0} | all-to-all | bytes 6291456 | tf_op jit(solution)/shard_map/all_to_all | solution.py:38
  127.8 4.4 %all-to-all-start.2 = ((bf16[8,1,96,2048]{3,2,1,0:T(8,128)(2,1)}), bf16[8,1,96,2048]{3,2,1,0:T(8,128)(2,1)}, u32[]{:S(2)}, u32[]{:S(2)}) async-start(bf16[8,1,96,2048]{3,2,1,0:T(8,128)(2,1)} %get-tuple-element.19), calls=%async_computation.2 | async-start | bytes 6291456 | tf_op jit(solution)/shard_map/all_to_all | solution.py:47
  132.4 6.9 %fusion.6 = f32[8,96,768]{2,1,0:T(8,128)} fusion(bf16[1,2048,768]{2,1,0:T(8,128)(2,1)} %param.12, bf16[8,1,96,2048]{3,2,1,0:T(8,128)(2,1)} %all_to_all.20), kind=kOutput, calls=%fused_computation.19 | convolution fusion | flops 2415919104 | bytes 8650752 | tf_op jit(solution)/shard_map/secd,edf->secf/dot_general | solution.py:40
  139.3 62.8 %all-to-all-done.2 = bf16[8,1,96,2048]{3,2,1,0:T(8,128)(2,1)} async-done(((bf16[8,1,96,2048]{3,2,1,0:T(8,128)(2,1)}), bf16[8,1,96,2048]{3,2,1,0:T(8,128)(2,1)}, u32[]{:S(2)}, u32[]{:S(2)}) %all-to-all-start.2) | async-done | bytes 3145760 | tf_op jit(solution)/shard_map/all_to_all | solution.py:47
  202.1 5.6 %fusion.1 = f32[8,96,768]{2,1,0:T(8,128)S(1)} fusion(bf16[8,1,96,2048]{3,2,1,0:T(8,128)(2,1)} %all-to-all-done.2, bf16[1,768,2048]{2,1,0:T(8,128)(2,1)} %param.13), kind=kOutput, calls=%fused_computation.14 | convolution fusion | flops 2415919104 | bytes 8650752 | tf_op jit(solution)/shard_map/secd,efd->secf/dot_general | solution.py:48
  207.7 4.6 %fusion.41 = (bf16[8,96,768]{2,1,0:T(8,128)(2,1)}, bf16[8,1,96,768]{3,2,0,1:T(8,128)(2,1)S(1)}, bf16[8,96,768]{2,1,0:T(8,128)(2,1)}) fusion(f32[8,96,768]{2,1,0:T(8,128)S(1)} %fusion.1, f32[8,96,768]{2,1,0:T(8,128)S(1)} %copy-done.4, bf16[1,2048,768]{2,1,0:T(8,128)(2,1)S(1)} %copy-done, bf16[8,1,96,2048]{3,2,1,0:T(8,128)(2,1)S(1)} %copy-done.1), kind=kOutput, calls=%fused_computation.52 | convolution fusion | flops 2424766464 | bytes 14548992 | tf_op jit(solution)/shard_map/secd,edf->secf/dot_general | solution.py:39
  212.3 1.0 copy-done.5
  213.3 4.1 fusion.22
  217.7 6.6 %fusion.25 = bf16[1,2048,768]{2,1,0:T(8,128)(2,1)} fusion(bf16[8,96,768]{2,1,0:T(8,128)(2,1)} %get-tuple-element.14, bf16[8,1,96,2048]{3,2,1,0:T(8,128)(2,1)} %all_to_all.20), kind=kOutput, calls=%fused_computation.33 | convolution fusion | flops 2417491968 | bytes 7471104 | tf_op jit(solution)/shard_map/secd,secf->edf/dot_general | solution.py:56
  224.4 4.3 %fusion.8 = f32[8,96,2048]{2,1,0:T(8,128)S(1)} fusion(bf16[1,2048,768]{2,1,0:T(8,128)(2,1)S(1)} %copy-done, bf16[8,1,96,768]{3,2,0,1:T(8,128)(2,1)} %copy-done.5), kind=kOutput, calls=%fused_computation.21 | convolution fusion | flops 2415919104 | bytes 10616832 | tf_op jit(solution)/shard_map/secf,edf->secd/dot_general | solution.py:58
  228.7 4.1 fusion.19
  232.8 4.5 %all-to-all-start.3 = ((bf16[8,1,96,2048]{3,2,1,0:T(8,128)(2,1)}), bf16[8,1,96,2048]{3,2,1,0:T(8,128)(2,1)}, u32[]{:S(2)}, u32[]{:S(2)}) async-start(bf16[8,1,96,2048]{3,2,1,0:T(8,128)(2,1)} %fusion.19), calls=%async_computation.3 | async-start | bytes 6291456 | tf_op jit(solution)/shard_map/all_to_all | solution.py:61
  237.3 6.7 %fusion.28 = bf16[1,768,2048]{2,1,0:T(8,128)(2,1)} fusion(bf16[8,96,768]{2,1,0:T(8,128)(2,1)} %get-tuple-element.16, bf16[8,1,96,2048]{3,2,1,0:T(8,128)(2,1)} %all-to-all-done.2), kind=kOutput, calls=%fused_computation.34 | convolution fusion | flops 2417491968 | bytes 7471104 | tf_op jit(solution)/shard_map/secf,secd->efd/dot_general | solution.py:49
  244.0 6.5 %fusion.16 = bf16[8,1,96,2048]{3,2,1,0:T(8,128)(2,1)} fusion(bf16[8,96,768]{2,1,0:T(8,128)(2,1)} %get-tuple-element.16, bf16[1,768,2048]{2,1,0:T(8,128)(2,1)} %param.13), kind=kOutput, calls=%fused_computation.30 | convolution fusion | flops 2417491968 | bytes 7471104 | tf_op jit(solution)/shard_map/secf,efd->secd/dot_general | solution.py:43
  250.5 56.7 %all-to-all-done.3 = bf16[8,1,96,2048]{3,2,1,0:T(8,128)(2,1)} async-done(((bf16[8,1,96,2048]{3,2,1,0:T(8,128)(2,1)}), bf16[8,1,96,2048]{3,2,1,0:T(8,128)(2,1)}, u32[]{:S(2)}, u32[]{:S(2)}) %all-to-all-start.3) | async-done | bytes 3145760 | tf_op jit(solution)/shard_map/all_to_all | solution.py:61
  307.1 4.7 %all-to-all-start.1 = ((bf16[8,1,96,2048]{3,2,1,0:T(8,128)(2,1)}), bf16[8,1,96,2048]{3,2,1,0:T(8,128)(2,1)}, u32[]{:S(2)}, u32[]{:S(2)}) async-start(bf16[8,1,96,2048]{3,2,1,0:T(8,128)(2,1)} %fusion.16), calls=%async_computation.1 | async-start | bytes 6291456 | tf_op jit(solution)/shard_map/all_to_all | solution.py:46
  311.9 2.2 convert_element_type.102
  314.0 7.5 %gather_fusion.3 = bf16[512,2048]{1,0:T(8,128)(2,1)} fusion(bf16[768,2048]{1,0:T(8,128)(2,1)} %bitcast.43, s32[1024]{0:T(1024)S(1)} %pad_clamp_fusion.1), kind=kCustom, calls=%fused_computation.3 | custom fusion | bytes 4196352 | tf_op jit(solution)/shard_map/gather | solution.py:66
  321.6 4.1 reshape.184
  325.7 56.4 %all-to-all-done.1 = bf16[8,1,96,2048]{3,2,1,0:T(8,128)(2,1)} async-done(((bf16[8,1,96,2048]{3,2,1,0:T(8,128)(2,1)}), bf16[8,1,96,2048]{3,2,1,0:T(8,128)(2,1)}, u32[]{:S(2)}, u32[]{:S(2)}) %all-to-all-start.1) | async-done | bytes 3145760 | tf_op jit(solution)/shard_map/all_to_all | solution.py:46
  382.0 7.5 %gather_fusion.1 = bf16[512,2048]{1,0:T(8,128)(2,1)} fusion(bf16[768,2048]{1,0:T(8,128)(2,1)} %bitcast.26, s32[1024]{0:T(1024)S(1)} %pad_clamp_fusion.1), kind=kCustom, calls=%fused_computation.1 | custom fusion | bytes 4196352 | tf_op jit(solution)/shard_map/gather | solution.py:62
  389.6 4.8 %reshape.185 = f32[128,4,2048]{2,1,0:T(4,128)} reshape(bf16[512,2048]{1,0:T(8,128)(2,1)} %gather_fusion.1) | data formatting | bytes 6291456 | tf_op jit(solution)/shard_map/convert_element_type | solution.py:63
  394.3 6.6 %multiply_reduce_fusion = (f32[128,4]{1,0:T(8,128)S(1)}, bf16[128,2048]{1,0:T(8,128)(2,1)}) fusion(f32[128,4,2048]{2,1,0:T(4,128)} %reshape.185, f32[128,2048]{1,0:T(8,128)} %convert_element_type.102, f32[128,4]{1,0:T(8,128)S(1)} %copy.19), kind=kLoop, calls=%fused_computation.10 | loop fusion | flops 3931648 | bytes 5771264 | tf_op jit(solution)/shard_map/reduce_sum | solution.py:65
  401.6 5.0 %reduce_sum.44 = bf16[128,2048]{1,0:T(8,128)(2,1)} reduce(bf16[128,4,2048]{2,1,0:T(4,128)(2,1)} %reshape.184, bf16[]{:T(256)} %constant.40.clone.1), dimensions={1}, to_apply=%region_5.6 | reduce | flops 786432 | bytes 2621442 | tf_op jit(solution)/shard_map/reduce_sum | solution.py:68
  (41 shorter events, 4.7 us)
Async XLA Ops:
  7.2 200.5 %copy-start = (bf16[1,2048,768]{2,1,0:T(8,128)(2,1)S(1)}, bf16[1,2048,768]{2,1,0:T(8,128)(2,1)}, u32[]{:S(2)}) copy-start(bf16[1,2048,768]{2,1,0:T(8,128)(2,1)} %param.11) | copy-start | bytes 9437188
  127.8 74.3 %all-to-all-start.2 = ((bf16[8,1,96,2048]{3,2,1,0:T(8,128)(2,1)}), bf16[8,1,96,2048]{3,2,1,0:T(8,128)(2,1)}, u32[]{:S(2)}, u32[]{:S(2)}) async-start(bf16[8,1,96,2048]{3,2,1,0:T(8,128)(2,1)} %get-tuple-element.19), calls=%async_computation.2 | async-start | bytes 6291456 | tf_op jit(solution)/shard_map/all_to_all | solution.py:47
  132.2 274.4 %reduce-scatter.4.cloned.1.call-start = ((), (), s32[]{:S(2)}) async-start(), calls=%async_computation.7 | async-start | bytes 3932160 | tf_op jit(solution)/shard_map/reduce_scatter | solution.py:70
  202.1 5.6 %copy-start.1 = (bf16[8,1,96,2048]{3,2,1,0:T(8,128)(2,1)S(1)}, bf16[8,1,96,2048]{3,2,1,0:T(8,128)(2,1)}, u32[]{:S(2)}) copy-start(bf16[8,1,96,2048]{3,2,1,0:T(8,128)(2,1)} %all_to_all.20) | copy-start | bytes 9437188
  202.1 5.7 %copy-start.4 = (f32[8,96,768]{2,1,0:T(8,128)S(1)}, f32[8,96,768]{2,1,0:T(8,128)}, u32[]{:S(2)}) copy-start(f32[8,96,768]{2,1,0:T(8,128)} %fusion.6) | copy-start | bytes 7077892
  212.3 1.0 copy-start.5
  217.4 189.1 %reduce-scatter.6.cloned.1.call-start = ((), (), s32[]{:S(2)}) async-start(), calls=%async_computation.8 | async-start | bytes 3932160 | tf_op jit(solution)/shard_map/reduce_scatter | solution.py:73
  224.3 4.3 %copy-start.2 = (bf16[1,2048,768]{2,1,0:T(8,128)(2,1)S(1)}, bf16[1,2048,768]{2,1,0:T(8,128)(2,1)}, u32[]{:S(2)}) copy-start(bf16[1,2048,768]{2,1,0:T(8,128)(2,1)} %param.12) | copy-start | bytes 9437188
  224.4 4.3 %copy-start.3 = (bf16[8,96,768]{2,1,0:T(8,128)(2,1)S(1)}, bf16[8,96,768]{2,1,0:T(8,128)(2,1)}, u32[]{:S(2)}) copy-start(bf16[8,96,768]{2,1,0:T(8,128)(2,1)} %get-tuple-element.14) | copy-start | bytes 3538948
  232.8 74.4 %all-to-all-start.3 = ((bf16[8,1,96,2048]{3,2,1,0:T(8,128)(2,1)}), bf16[8,1,96,2048]{3,2,1,0:T(8,128)(2,1)}, u32[]{:S(2)}, u32[]{:S(2)}) async-start(bf16[8,1,96,2048]{3,2,1,0:T(8,128)(2,1)} %fusion.19), calls=%async_computation.3 | async-start | bytes 6291456 | tf_op jit(solution)/shard_map/all_to_all | solution.py:61
  237.2 169.3 %reduce-scatter.8.cloned.1.call-start = ((), (), s32[]{:S(2)}) async-start(), calls=%async_computation.9 | async-start | bytes 3932160 | tf_op jit(solution)/shard_map/reduce_scatter | solution.py:76
  307.1 74.9 %all-to-all-start.1 = ((bf16[8,1,96,2048]{3,2,1,0:T(8,128)(2,1)}), bf16[8,1,96,2048]{3,2,1,0:T(8,128)(2,1)}, u32[]{:S(2)}, u32[]{:S(2)}) async-start(bf16[8,1,96,2048]{3,2,1,0:T(8,128)(2,1)} %fusion.16), calls=%async_computation.1 | async-start | bytes 6291456 | tf_op jit(solution)/shard_map/all_to_all | solution.py:46
Sparse Core Ops, SparseCore 0:
  217.6 37.0 reduce-scatter.3
  257.9 37.9 reduce-scatter.5
  299.0 37.9 reduce-scatter.7
where the time goes:
time: 421 us; the launch traced here: 414 us
  waiting for transfers between devices  176 us (42%)
  blocking collectives  77.9 us (19%)
  local copies, waits for them, and re-layouts  57.4 us (14%)
  matrix products  49.3 us (12%)
  other arithmetic  24.7 us (6%)
  between operations  14.3 us (3%)
  starting transfers between devices  14.1 us (3%)
    all_to_all x1, blocking collectives, per_device(): lax.all_to_all(outgoing, 'expert', split_axis=0, concat_axis=0, tiled=True)  77.9 us
    all_to_all x1, waiting for transfers between devices, per_device(): lax.all_to_all(outgoing_grad, 'expert', split_axis=0, concat_axis=0, tile...  62.8 us
    all_to_all x1, waiting for transfers between devices, per_device(): lax.all_to_all(d_rows, 'expert', split_axis=0, concat_axis=0, tiled=True)  56.7 us
    all_to_all x1, waiting for transfers between devices, per_device(): lax.all_to_all(produced, 'expert', split_axis=0, concat_axis=0, tiled=True)  56.4 us
    mul x2, local copies, waits for them, and re-layouts, per_device(): combine[:, :, None] * cot_float[:, None, :]  9.45 us
    gather x1, local copies, waits for them, and re-layouts, per_device(): scaled[pair_index]  8.96 us
  transfers between devices with their start and end apart: 6, of which 3 were waited for; matrix products, arithmetic and copies ran while one was open for 18% of the time, Pallas kernels for 0%

commit v1 on v0

v1 whole, which is shorter than its diff:
```python
import jax
import jax.numpy as jnp
from jax import lax
from jax.sharding import PartitionSpec as P


def per_device(tokens, routes, combine, cotangent, w_gate, w_up, w_down):
    tok_rows, features = tokens.shape
    groups = lax.axis_size("expert")
    experts = w_gate.shape[0] * groups
    mine = lax.axis_index("expert")
    bf16 = jnp.bfloat16
    f32 = jnp.float32
    chosen = routes[:, :, None] == jnp.arange(experts, dtype=jnp.int32)[None, None, :]
    weights = jnp.sum(jnp.where(chosen, combine[:, :, None], 0.0), axis=1)
    all_weights = lax.all_gather(weights, "expert", axis=0, tiled=True)
    weight = lax.dynamic_slice_in_dim(all_weights, mine, 1, axis=1)
    all_tokens = lax.all_gather(tokens, "expert", axis=0, tiled=True)
    all_cot = lax.all_gather(cotangent, "expert", axis=0, tiled=True)
    wg, wu, wd = w_gate[0], w_up[0], w_down[0]
    gate_pre = jnp.dot(all_tokens, wg, preferred_element_type=f32)
    up_pre = jnp.dot(all_tokens, wu, preferred_element_type=f32)
    sig = jax.nn.sigmoid(gate_pre)
    act = gate_pre * sig
    hidden = act * up_pre
    scaled = (hidden * weight).astype(bf16)
    out_part = jnp.dot(scaled, wd, preferred_element_type=f32).astype(bf16)
    output = lax.psum_scatter(out_part, "expert", scatter_dimension=0, tiled=True)
    d_raw = jnp.einsum("td,fd->tf", all_cot, wd, preferred_element_type=f32)
    d_comb = jnp.sum(hidden * d_raw, axis=1)
    d_hidden = d_raw * weight
    d_gate = (d_hidden * up_pre * sig * (1.0 + gate_pre * (1.0 - sig))).astype(bf16)
    d_up = (d_hidden * act).astype(bf16)
    d_rows = (
        jnp.einsum("tf,df->td", d_gate, wg, preferred_element_type=f32)
        + jnp.einsum("tf,df->td", d_up, wu, preferred_element_type=f32)
    ).astype(bf16)
    d_tokens = lax.psum_scatter(d_rows, "expert", scatter_dimension=0, tiled=True)
    part_down = jnp.einsum("tf,td->fd", scaled, all_cot, preferred_element_type=f32).astype(bf16)
    part_gate = jnp.einsum("td,tf->df", all_tokens, d_gate, preferred_element_type=f32).astype(bf16)
    part_up = jnp.einsum("td,tf->df", all_tokens, d_up, preferred_element_type=f32).astype(bf16)
    d_w_down = lax.psum_scatter(part_down, "dp", scatter_dimension=1, tiled=True)[None]
    d_w_gate = lax.psum_scatter(part_gate, "dp", scatter_dimension=0, tiled=True)[None]
    d_w_up = lax.psum_scatter(part_up, "dp", scatter_dimension=0, tiled=True)[None]
    back = lax.all_to_all(
        d_comb.reshape(groups, tok_rows), "expert", split_axis=0, concat_axis=0, tiled=True
    )
    d_combine = jnp.sum(jnp.where(chosen, back.T[:, None, :], 0.0), axis=2)
    return output, d_tokens, d_combine, d_w_gate, d_w_up, d_w_down


def solution(mesh):
    rows = P(("dp", "expert"), None)
    return jax.shard_map(
        per_device,
        mesh=mesh,
        in_specs=(rows, rows, rows, rows) + (P("expert", None, None),) * 3,
        out_specs=(
            rows,
            rows,
            rows,
            P("expert", "dp", None),
            P("expert", "dp", None),
            P("expert", None, "dp"),
        ),
        check_vma=False,
    )
```

time: 421 us -> 530 us (1.26); the launches traced: 414 us -> 530 us
  waiting for transfers between devices: 176 us -> 408 us
  local copies, waits for them, and re-layouts: 57.4 us -> 5.78 us
  blocking collectives: 77.9 us -> 30.4 us
  other arithmetic: 24.7 us -> 6.76 us
  matrix products: 49.3 us -> 60.6 us
  starting transfers between devices: 14.1 us -> 4 us
    reduce_scatter x3 -> x5, waiting for transfers between devices: 0.01 us -> 263 us  [the longest x1 92.4 us: per_device(): lax.psum_scatter(out_part, 'expert', scatter_dimension=0, tiled=True)]
    all_to_all x3 -> x1, waiting for transfers between devices: 176 us -> 6.27 us  [per_device(): lax.all_to_all(d_comb.reshape(groups, tok_rows), 'expert', split_axis=0,...]
    all_gather x0 -> x2, waiting for transfers between devices: none -> 138 us  [the longest x1 77.6 us: per_device(): all_tokens = lax.all_gather(tokens, 'expert', axis=0, tiled=True)]
    all_to_all x1 -> x0, blocking collectives: 77.9 us -> none  [per_device(): lax.all_to_all(outgoing, 'expert', split_axis=0, concat_axis=0, tiled=True)]
    gather x4 -> x0, local copies, waits for them, and re-layouts: 32.3 us -> none  [the longest x1 8.96 us: per_device(): scaled[pair_index]]
    all_gather x0 -> x1, blocking collectives: none -> 30.4 us  [per_device(): all_weights = lax.all_gather(weights, 'expert', axis=0, tiled=True)]
    dot_general x9, matrix products: 49.3 us -> 60.6 us  [the longest x1 8.8 us: per_device(): d_raw = jnp.einsum('td,fd->tf', all_cot, wd, preferred_element_type=f32)]
    reduce_sum x3 -> x1, other arithmetic: 11.7 us -> 0.6 us  [per_device(): d_combine = jnp.sum(jnp.where(chosen, back.T[:, None, :], 0.0), axis=2)]
  transfers between devices with their start and end apart: 6 -> 8, of which waited for: 3 -> 8; matrix products, arithmetic and copies ran while one was open for 18% -> 10% of each run, Pallas kernels for 0% -> 0%
where the time goes in v1:
time: 530 us
  waiting for transfers between devices  408 us (77%)
  matrix products  60.6 us (11%)
  blocking collectives  30.4 us (6%)
  between operations  14.2 us (3%)
  other arithmetic  6.76 us (1%)
  local copies, waits for them, and re-layouts  5.78 us (1%)
    reduce_scatter x1, waiting for transfers between devices, per_device(): lax.psum_scatter(out_part, 'expert', scatter_dimension=0, tiled=True)  92.4 us
    reduce_scatter x1, waiting for transfers between devices, per_device(): lax.psum_scatter(d_rows, 'expert', scatter_dimension=0, tiled=True)  91.9 us
    all_gather x1, waiting for transfers between devices, per_device(): all_tokens = lax.all_gather(tokens, 'expert', axis=0, tiled=True)  77.6 us
    all_gather x1, waiting for transfers between devices, per_device(): all_cot = lax.all_gather(cotangent, 'expert', axis=0, tiled=True)  60.1 us
    reduce_scatter x1, waiting for transfers between devices, per_device(): lax.psum_scatter(part_down, 'dp', scatter_dimension=1, tiled=True)[None]  38.6 us
    reduce_scatter x1, waiting for transfers between devices, per_device(): lax.psum_scatter(part_up, 'dp', scatter_dimension=0, tiled=True)[None]  38.2 us
    all_gather x1, blocking collectives, per_device(): all_weights = lax.all_gather(weights, 'expert', axis=0, tiled=True)  30.4 us
  transfers between devices with their start and end apart: 8, of which 8 were waited for; matrix products, arithmetic and copies ran while one was open for 10% of the time, Pallas kernels for 0%

profile of v1, /device:TPU:0, one launch (start us, length us, event | category | flops | bytes accessed | tf_op | source)
XLA Modules:
  0.0 529.7 jit_solution(10628203615000590273)
XLA Ops:
  7.2 0.7 all-gather.3.cloned.1.call-update
  7.9 0.0 all-gather.5.cloned.1.call-start
  8.0 0.7 all-gather.5.cloned.1.call-update
  8.7 77.6 %all-gather.3.cloned.1.call-done = bf16[1024,2048]{1,0:T(8,128)(2,1)} async-done(((bf16[128,2048]{1,0:T(8,128)(2,1)}), bf16[1024,2048]{1,0:T(8,128)(2,1)}) %all-gather.3.cloned.1.call-update) | async-done | bytes 4194320 | tf_op jit(solution)/shard_map/all_gather | solution.py:18
  86.3 8.5 %fusion.4 = f32[1024,768]{0,1:T(8,128)} fusion(bf16[1024,2048]{1,0:T(8,128)(2,1)} %all-gather.3.cloned.1.call-done, bf16[1,2048,768]{2,1,0:T(8,128)(2,1)} %param.12), kind=kOutput, calls=%fused_computation.9 | convolution fusion | flops 3221225472 | bytes 10485760 | tf_op jit(solution)/shard_map/dot_general | solution.py:22
  94.8 5.2 fusion.8
  100.0 60.1 %all-gather.5.cloned.1.call-done = bf16[1024,2048]{1,0:T(8,128)(2,1)} async-done(((bf16[128,2048]{1,0:T(8,128)(2,1)}), bf16[1024,2048]{1,0:T(8,128)(2,1)}) %all-gather.5.cloned.1.call-update) | async-done | bytes 4194320 | tf_op jit(solution)/shard_map/all_gather | solution.py:19
  160.1 8.8 %multiply_reduce_fusion = (f32[1024]{0:T(1024)}, f32[1024,768]{0,1:T(8,128)}) fusion(f32[1024,768]{0,1:T(8,128)} %fusion.4, f32[1024,768]{0,1:T(8,128)} %fusion.8, bf16[1024,2048]{1,0:T(8,128)(2,1)} %all-gather.5.cloned.1.call-done, bf16[1,768,2048]{2,1,0:T(8,128)(2,1)S(1)} %copy-done), kind=kOutput, calls=%fused_computation.15 | convolution fusion | flops 3226729472 | bytes 16781312 | tf_op jit(solution)/shard_map/td,fd->tf/dot_general | solution.py:29
  168.9 3.3 all-to-all-start
  172.2 0.0 reduce-scatter.10.cloned.1.call-start
  172.3 6.3 %all-to-all-done = f32[8,1,128]{2,1,0:T(1,128)S(1)} async-done(((f32[8,1,128]{2,1,0:T(1,128)}), f32[8,1,128]{2,1,0:T(1,128)S(1)}, u32[]{:S(2)}, u32[]{:S(2)}) %all-to-all-start) | async-done | bytes 4128 | tf_op jit(solution)/shard_map/all_to_all | solution.py:45
  178.5 0.6 select_reduce_fusion
  179.1 30.4 %all_gather.10 = f32[1024,8]{0,1:T(8,128)S(1)} all-gather(f32[128,8]{0,1:T(8,128)S(1)} %get-tuple-element.31), channel_id=1, replica_groups=mesh['dp'=4,'expert'=8] {'expert'}, dimensions={0}, use_global_device_ids=true | all-gather | bytes 36864 | tf_op jit(solution)/shard_map/all_gather | solution.py:16
  209.6 6.2 %multiply_convert_fusion = (bf16[1024,768]{0,1:T(8,128)(2,1)}, bf16[1024,768]{0,1:T(8,128)(2,1)S(1)}, bf16[1024,768]{0,1:T(8,128)(2,1)}) fusion(f32[1024,768]{0,1:T(8,128)} %get-tuple-element.36, f32[1024]{0:T(1024)S(1)} %bitcast.46, f32[1024,768]{0,1:T(8,128)} %fusion.8, f32[1024,768]{0,1:T(8,128)} %fusion.4), kind=kLoop, calls=%fused_computation.16 | loop fusion | flops 13369344 | bytes 14159872 | tf_op jit(solution)/shard_map/convert_element_type | solution.py:33
  215.7 1.2 copy-done.2
  216.9 4.8 fusion.11
  221.7 0.2 reduce-scatter.12.cloned.1.call-start
  221.9 7.9 %fusion.12 = bf16[2048,768]{0,1:T(8,128)(2,1)} fusion(bf16[1024,768]{0,1:T(8,128)(2,1)} %get-tuple-element.32, bf16[1024,2048]{1,0:T(8,128)(2,1)} %all-gather.3.cloned.1.call-done), kind=kOutput, calls=%fused_computation.22 | convolution fusion | flops 3222798336 | bytes 8912896 | tf_op jit(solution)/shard_map/td,tf->df/dot_general | solution.py:41
  229.8 0.0 reduce-scatter.14.cloned.1.call-start
  229.9 7.8 %convolution_convert_fusion.1 = bf16[768,2048]{1,0:T(8,128)(2,1)} fusion(bf16[1024,768]{0,1:T(8,128)(2,1)} %get-tuple-element.34, bf16[1024,2048]{1,0:T(8,128)(2,1)} %all-gather.5.cloned.1.call-done), kind=kOutput, calls=%fused_computation.2 | convolution fusion | flops 3222798336 | bytes 8912896 | tf_op jit(solution)/shard_map/tf,td->fd/dot_general | solution.py:39
  237.7 0.0 reduce-scatter.6.cloned.1.call-start
  237.7 6.5 %convolution_convert_fusion = bf16[1024,2048]{1,0:T(8,128)(2,1)} fusion(bf16[1024,768]{0,1:T(8,128)(2,1)} %get-tuple-element.34, bf16[1,768,2048]{2,1,0:T(8,128)(2,1)S(1)} %copy-done), kind=kOutput, calls=%fused_computation.1 | convolution fusion | flops 3223322624 | bytes 8912896 | tf_op jit(solution)/shard_map/dot_general | solution.py:27
  244.2 0.3 reduce-scatter.8.cloned.1.call-start
  244.5 6.0 %fusion.6 = f32[1024,2048]{1,0:T(8,128)S(1)} fusion(bf16[1024,768]{0,1:T(8,128)(2,1)} %copy-done.2, bf16[1,2048,768]{2,1,0:T(8,128)(2,1)} %param.11), kind=kOutput, calls=%fused_computation.11 | convolution fusion | flops 3221225472 | bytes 13107200 | tf_op jit(solution)/shard_map/tf,df->td/dot_general | solution.py:35
  250.5 5.2 add_convert_fusion
  255.7 1.3 reduce-scatter.10.cloned.1.call-done
  257.1 2.3 copy.29
  259.4 38.2 %reduce-scatter.12.cloned.1.call-done = bf16[512,768]{0,1:T(8,128)(2,1)} async-done(((bf16[2048,768]{0,1:T(8,128)(2,1)}), bf16[512,768]{0,1:T(8,128)(2,1)}) %reduce-scatter.12.cloned.1.call-update) | async-done | bytes 786448 | tf_op jit(solution)/shard_map/reduce_scatter | solution.py:44
  297.6 2.3 copy.30
  299.9 38.6 %reduce-scatter.14.cloned.1.call-done = bf16[768,512]{1,0:T(8,128)(2,1)} async-done(((bf16[768,2048]{1,0:T(8,128)(2,1)}), bf16[768,512]{1,0:T(8,128)(2,1)}) %reduce-scatter.14.cloned.1.call-update) | async-done | bytes 786448 | tf_op jit(solution)/shard_map/reduce_scatter | solution.py:42
  338.5 92.4 %reduce-scatter.6.cloned.1.call-done = bf16[128,2048]{1,0:T(8,128)(2,1)} async-done(((bf16[1024,2048]{1,0:T(8,128)(2,1)}), bf16[128,2048]{1,0:T(8,128)(2,1)}) %reduce-scatter.6.cloned.1.call-update) | async-done | bytes 524304 | tf_op jit(solution)/shard_map/reduce_scatter | solution.py:28
  430.9 91.9 %reduce-scatter.8.cloned.1.call-done = bf16[128,2048]{1,0:T(8,128)(2,1)} async-done(((bf16[1024,2048]{1,0:T(8,128)(2,1)}), bf16[128,2048]{1,0:T(8,128)(2,1)}) %reduce-scatter.8.cloned.1.call-update) | async-done | bytes 524304 | tf_op jit(solution)/shard_map/reduce_scatter | solution.py:38
  (24 shorter events, 0.2 us)
Async XLA Ops:
  7.2 152.9 %copy-start = (bf16[1,768,2048]{2,1,0:T(8,128)(2,1)S(1)}, bf16[1,768,2048]{2,1,0:T(8,128)(2,1)}, u32[]{:S(2)}) copy-start(bf16[1,768,2048]{2,1,0:T(8,128)(2,1)} %param.13) | copy-start | bytes 9437188
  7.2 79.1 %all-gather.3.cloned.1.call-start = ((), (), s32[]{:S(2)}) async-start(), calls=%async_computation.6 | async-start | bytes 4718592 | tf_op jit(solution)/shard_map/all_gather | solution.py:18
  7.9 152.2 %all-gather.5.cloned.1.call-start = ((), (), s32[]{:S(2)}) async-start(), calls=%async_computation.8 | async-start | bytes 4718592 | tf_op jit(solution)/shard_map/all_gather | solution.py:19
  86.3 8.5 %copy-start.5 = (bf16[1024,2048]{1,0:T(8,128)(2,1)S(1)}, bf16[1024,2048]{1,0:T(8,128)(2,1)}, u32[]{:S(2)}) copy-start(bf16[1024,2048]{1,0:T(8,128)(2,1)} %all-gather.3.cloned.1.call-done) | copy-start | bytes 12582916
  86.3 8.5 %copy-start.7 = (bf16[1,2048,768]{2,1,0:T(8,128)(2,1)S(1)}, bf16[1,2048,768]{2,1,0:T(8,128)(2,1)}, u32[]{:S(2)}) copy-start(bf16[1,2048,768]{2,1,0:T(8,128)(2,1)} %param.11) | copy-start | bytes 9437188
  100.0 78.5 %copy-start.3 = (s32[128,4]{0,1:T(4,128)S(1)}, s32[128,4]{0,1:T(4,128)}, u32[]{:S(2)}) copy-start(s32[128,4]{0,1:T(4,128)} %param.8) | copy-start | bytes 6148
  100.0 78.5 %copy-start.4 = (f32[128,4]{0,1:T(4,128)S(1)}, f32[128,4]{0,1:T(4,128)}, u32[]{:S(2)}) copy-start(f32[128,4]{0,1:T(4,128)} %param.9) | copy-start | bytes 6148
  168.9 9.6 %all-to-all-start = ((f32[8,1,128]{2,1,0:T(1,128)}), f32[8,1,128]{2,1,0:T(1,128)S(1)}, u32[]{:S(2)}, u32[]{:S(2)}) async-start(f32[8,1,128]{2,1,0:T(1,128)} %bitcast.5), calls=%async_computation.2 | async-start | bytes 8192 | tf_op jit(solution)/shard_map/all_to_all | solution.py:45
  172.2 84.9 %reduce-scatter.10.cloned.1.call-start = ((), (), s32[]{:S(2)}) async-start(), calls=%async_computation.10 | async-start | bytes 3932160 | tf_op jit(solution)/shard_map/reduce_scatter | solution.py:43
  209.5 7.3 %copy-start.6 = (bf16[1024,2048]{1,0:T(8,128)(2,1)S(1)}, bf16[1024,2048]{1,0:T(8,128)(2,1)}, u32[]{:S(2)}) copy-start(bf16[1024,2048]{1,0:T(8,128)(2,1)} %all-gather.3.cloned.1.call-done) | copy-start | bytes 12582916
  215.7 1.2 copy-start.2
  221.7 75.9 %reduce-scatter.12.cloned.1.call-start = ((), (), s32[]{:S(2)}) async-start(), calls=%async_computation.11 | async-start | bytes 3932160 | tf_op jit(solution)/shard_map/reduce_scatter | solution.py:44
  229.8 108.7 %reduce-scatter.14.cloned.1.call-start = ((), (), s32[]{:S(2)}) async-start(), calls=%async_computation.12 | async-start | bytes 3932160 | tf_op jit(solution)/shard_map/reduce_scatter | solution.py:42
  237.7 193.2 %reduce-scatter.6.cloned.1.call-start = ((), (), s32[]{:S(2)}) async-start(), calls=%async_computation.7 | async-start | bytes 4718592 | tf_op jit(solution)/shard_map/reduce_scatter | solution.py:28
  244.2 278.6 %reduce-scatter.8.cloned.1.call-start = ((), (), s32[]{:S(2)}) async-start(), calls=%async_computation.9 | async-start | bytes 4718592 | tf_op jit(solution)/shard_map/reduce_scatter | solution.py:38
  244.5 6.0 %copy-start.1 = (bf16[1024,768]{0,1:T(8,128)(2,1)S(1)}, bf16[1024,768]{0,1:T(8,128)(2,1)}, u32[]{:S(2)}) copy-start(bf16[1024,768]{0,1:T(8,128)(2,1)} %get-tuple-element.32) | copy-start | bytes 4718596
  244.5 6.0 %copy-start.8 = (bf16[1,2048,768]{2,1,0:T(8,128)(2,1)S(1)}, bf16[1,2048,768]{2,1,0:T(8,128)(2,1)}, u32[]{:S(2)}) copy-start(bf16[1,2048,768]{2,1,0:T(8,128)(2,1)} %param.12) | copy-start | bytes 9437188
Sparse Core Ops, SparseCore 0:
  10.1 76.0 all-gather.2
  88.4 71.6 all-gather.4
  221.8 35.2 reduce-scatter.9
  259.6 37.9 reduce-scatter.11
  300.6 37.9 reduce-scatter.13
  343.0 87.8 reduce-scatter.5
  435.1 87.6 reduce-scatter.7
